TPU v7x, 32 devices: a whole 2x2x4 slice. The times are simulated.
32 devices in a mesh: region: 2 (over core), space: 16 (over z, y, x).
Axes of the slice: x: 2, y: 2, z: 4, core: 2. Of those that a mesh axis runs over, the one named last changes fastest.
Arguments:
- f_cells: float32 [2, 128, 128, 128], P('region', 'space'), may hold values from -6 to 6
- g_mortar: float32 [2, 4096], P('region', 'space'), may hold values from -6 to 6
- mask_cells: int32 [2, 128, 128, 128], P('region', 'space'), may hold values 0 or 1
- zone_ids: int32 [2, 128, 128, 128], P('region', 'space'), may hold values from 0 to 15
- zone_coef: float32 [16], replicated, may hold values from 0.02 to 2
- mort_index: int32 [16, 2048], P('space'), may hold values from 0 to 511
- face_stokes: int32 [16, 2048], P('space'), may hold values from 0 to 1023
- face_darcy: int32 [16, 2048], P('space'), may hold values from 0 to 1023
- mort_weight: float32 [16, 2048], P('space'), may hold values from 0.25 to 1
- tile_count: int32 [16, 16], P('space'), may hold values from 1 to 128, as said below
Outputs:
- solution_cells: float32 [2, 128, 128, 128], P('region', 'space')
- solution_mortar: float32 [2, 4096], P('region', 'space')
Inputs may be any that keep to these rules, and one draw needn't show every extreme that they name: `tile_count`: in every slab pair some tile has all 128 rows valid.
All inputs are finite; a program needn't handle non-finite values. No bound on the sum of `mask_cells` on one device may be relied on, other than what follows from the above.
Results may differ from a plain program's by a relative error of at most 0.00011.
Values sent between devices are 32-bit elements; how exact they have to be, the bound alone decides.
A program may use at most 64 MiB of HBM per device.

v0:
```python
import jax
import jax.numpy as jnp
from jax import lax
from jax.sharding import PartitionSpec as P

ZONES = 16
ITERS = 4


OMEGA = 0.8
STAB = 0.05


def padded_2(x, sides, width):
    for axis, dim in sides:
        devices, length = (lax.axis_size(axis), x.shape[dim])
        up = [(i, (i + 1) % devices) for i in range(devices - 1)]
        down = [(j, i) for i, j in up]
        last = lax.slice_in_dim(x, length - width, length, axis=dim)
        first = lax.slice_in_dim(x, 0, width, axis=dim)
        before = lax.ppermute(last, axis, up)
        after = lax.ppermute(first, axis, down)
        x = jnp.concatenate([before, x, after], axis=dim)
    return x


def stencil_sum(padded):
    total = padded[:, 2:, 1:-1, 1:-1] + padded[:, :-2, 1:-1, 1:-1]
    total = total + padded[:, 1:-1, 2:, 1:-1] + padded[:, 1:-1, :-2, 1:-1]
    return total + padded[:, 1:-1, 1:-1, 2:] + padded[:, 1:-1, 1:-1, :-2]


def side_pad(values):
    return jnp.pad(values, ((0, 0), (0, 0), (1, 1), (1, 1)))


def fine_neighbours(values):
    padded = padded_2(values, (("space", 1),), 1)
    return stencil_sum(side_pad(padded))


def coarse_neighbours(values):
    padded = padded_2(values, (("space", 1),), 1)
    return stencil_sum(side_pad(padded))


def fine_apply(cells, active, react):
    return (
        active * ((6.0 + react) * cells - fine_neighbours(active * cells)) + (1.0 - active) * cells
    )


def coarsen(values):
    values = values[:, 0::2] + values[:, 1::2]
    values = values[:, :, 0::2] + values[:, :, 1::2]
    return values[:, :, :, 0::2] + values[:, :, :, 1::2]


def refine(values):
    return jnp.repeat(jnp.repeat(jnp.repeat(values, 2, axis=1), 2, axis=2), 2, axis=3)


def vcycle(resid, active, react, fine_diag, coarse_diag):
    first = OMEGA * resid / fine_diag
    first_image = fine_apply(first, active, react)
    coarse_rhs = coarsen(resid - first_image)
    sweep = OMEGA * coarse_rhs / coarse_diag
    coarse_res = coarse_rhs - (coarse_diag * sweep - 2.0 * coarse_neighbours(sweep))
    sweep = sweep + OMEGA * coarse_res / coarse_diag
    second = first + refine(sweep)
    second_image = fine_apply(second, active, react)
    return second + OMEGA * (resid - second_image) / fine_diag


def combine(first, second, scale_one, scale_two):
    return (
        scale_one * first[0] + scale_two * second[0],
        scale_one * first[1] + scale_two * second[1],
    )


def local_inner(first, second):
    return jnp.sum(first[0] * second[0]) + jnp.sum(first[1] * second[1])


def global_inner(first, second):
    return lax.psum(local_inner(first, second), ("region", "space"))


def rotation(alpha_now, beta_now, cosine, sine_val, delta_bar, epsilon, phi_bar):
    old_eps = epsilon
    delta_val = cosine * delta_bar + sine_val * alpha_now
    gamma_bar = sine_val * delta_bar - cosine * alpha_now
    epsilon = sine_val * beta_now
    delta_bar = -cosine * beta_now
    gamma_val = jnp.sqrt(gamma_bar * gamma_bar + beta_now * beta_now)
    cosine = gamma_bar / gamma_val
    sine_val = beta_now / gamma_val
    phi_step = cosine * phi_bar
    phi_bar = sine_val * phi_bar
    return (old_eps, delta_val, gamma_val, phi_step, cosine, sine_val, delta_bar, epsilon, phi_bar)


def on_device(
    f_cells,
    g_mortar,
    mask_cells,
    zone_ids,
    zone_coef,
    mort_index,
    face_stokes,
    face_darcy,
    mort_weight,
    tile_count,
):
    region_index = lax.axis_index("region")
    side_sign = 1.0 - 2.0 * region_index.astype(jnp.float32)
    slab_x = f_cells.shape[1]
    slab_y = f_cells.shape[2]
    depth = f_cells.shape[3]
    face_count = slab_x * slab_y
    mort_count = g_mortar.shape[1]
    layer = region_index * (depth - 1)
    active = mask_cells.astype(jnp.float32)
    react = jnp.zeros(f_cells.shape, jnp.float32)
    for zone in range(ZONES):
        react = jnp.where(zone_ids == zone, zone_coef[zone], react)
    fine_diag = active * (6.0 + react) + (1.0 - active)
    coarse_diag = 2.0 * (6.0 + 0.125 * coarsen(active * react))
    rows_iota = jnp.arange(mort_index.shape[1], dtype=jnp.int32)
    valid = (rows_iota % 128)[None, :] < jnp.repeat(tile_count, 128, axis=1)
    margin_coef = jnp.where(valid, mort_weight, 0.0)[0]
    mort_list = mort_index[0]
    stokes_list = face_stokes[0]
    darcy_list = face_darcy[0]
    own_list = jnp.where(region_index == 0, stokes_list, darcy_list)
    depth_mask = (lax.broadcasted_iota(jnp.int32, (1, 1, 1, depth), 3) == layer).astype(jnp.float32)
    diag_full = jax.ops.segment_sum(
        margin_coef * margin_coef, mort_list, num_segments=2 * mort_count
    )
    mort_diag = (
        STAB + lax.dynamic_slice_in_dim(diag_full, region_index * mort_count, mort_count) / 3.0
    )[None, :]

    def precondition(vector):
        return (vcycle(vector[0], active, react, fine_diag, coarse_diag), vector[1] / mort_diag)

    rhs = (f_cells, g_mortar)
    lanczos_old = rhs
    lanczos_new = rhs
    work_vec = precondition(rhs)
    old_beta = jnp.zeros((), jnp.float32)
    delta_bar = jnp.zeros((), jnp.float32)
    epsilon = jnp.zeros((), jnp.float32)
    cosine = jnp.full((), -1.0, jnp.float32)
    sine_val = jnp.zeros((), jnp.float32)
    search = (jnp.zeros_like(f_cells), jnp.zeros_like(g_mortar))
    search_two = search
    solution = search
    beta_now = jnp.sqrt(global_inner(rhs, work_vec))
    phi_bar = beta_now
    for iteration in range(ITERS):
        basis = (work_vec[0] / beta_now, work_vec[1] / beta_now)
        cells, mults = basis
        face_cells = lax.dynamic_index_in_dim(cells[0], layer, axis=2, keepdims=False).reshape(-1)
        partial_value = jax.ops.segment_sum(
            side_sign * margin_coef * face_cells[own_list], mort_list, num_segments=2 * mort_count
        )
        mortar_rows = lax.psum_scatter(partial_value, "region", scatter_dimension=0, tiled=True)
        paired = lax.all_gather(mults, "region", axis=0, tiled=True).reshape(-1)
        face_add = jax.ops.segment_sum(
            side_sign * margin_coef * paired[mort_list], own_list, num_segments=face_count
        )
        field = (
            fine_apply(cells, active, react) + face_add.reshape(1, slab_x, slab_y, 1) * depth_mask
        )
        image = (field, mortar_rows[None, :] - STAB * mults)
        if iteration > 0:
            image = combine(image, lanczos_old, 1.0, -(beta_now / old_beta))
        alpha_now = global_inner(basis, image)
        image = combine(image, lanczos_new, 1.0, -(alpha_now / beta_now))
        lanczos_old = lanczos_new
        lanczos_new = image
        work_vec = precondition(lanczos_new)
        old_beta = beta_now
        beta_now = jnp.sqrt(global_inner(lanczos_new, work_vec))
        old_eps, delta_val, gamma_val, phi_step, cosine, sine_val, delta_bar, epsilon, phi_bar = (
            rotation(alpha_now, beta_now, cosine, sine_val, delta_bar, epsilon, phi_bar)
        )
        search_one = search_two
        search_two = search
        search = (
            (basis[0] - old_eps * search_one[0] - delta_val * search_two[0]) / gamma_val,
            (basis[1] - old_eps * search_one[1] - delta_val * search_two[1]) / gamma_val,
        )
        solution = (solution[0] + phi_step * search[0], solution[1] + phi_step * search[1])
    return (solution[0], solution[1])


def solution(mesh):
    in_specs = (
        P("region", "space", None, None),
        P("region", "space"),
        P("region", "space", None, None),
        P("region", "space", None, None),
        P(),
        P("space", None),
        P("space", None),
        P("space", None),
        P("space", None),
        P("space", None),
    )
    out_specs = (P("region", "space", None, None), P("region", "space"))
    return jax.shard_map(
        on_device, mesh=mesh, in_specs=in_specs, out_specs=out_specs, check_vma=False
    )
```

profile of v0, /device:TPU:0, one launch (start us, length us, event | category | flops | bytes accessed | tf_op | source)
XLA Modules:
  0.0 1219.6 jit_solution(8048382856444145897)
XLA Ops:
  36.6 14.7 %scatter_custom_fusion = f32[512]{0:T(512)S(1)} fusion(s32[2048]{0:T(1024)S(1)} %bitcast.156, f32[2048]{0:T(1024)S(1)} %bitcast.152, f32[]{:T(128)} %constant.32.clone.1), kind=kCustom, calls=%fused_computation.417 | custom fusion | flops 2048 | bytes 2052 | tf_op jit(solution)/shard_map/scatter-add | solution.py:138
  106.7 12.7 %multiply_reduce_fusion.7 = (f32[]{:T(128)}, f32[1,8,128,128]{2,1,3,0:T(8,128)}) fusion(f32[1,8,128,128]{2,1,3,0:T(8,128)S(1)} %copy.70, f32[1,10,130,130]{2,1,3,0:T(8,128)S(1)} %select_maximum_fusion.24, f32[1,8,128,128]{2,1,3,0:T(8,128)S(1)} %convert_multiply_fusion.12, f32[1,1,128,128]{2,1,3,0:T(1,128)S(1)} %collective-permute-done.5, ...), kind=kLoop, calls=%fused_computation.246 | loop fusion | flops 7602175 | bytes 5111876 | tf_op jit(solution)/shard_map/reduce_sum | solution.py:83
  121.2 46.7 %psum.63 = f32[]{:T(128)} all-reduce(f32[]{:T(128)S(6)} %add.754), channel_id=1, replica_groups=mesh['region'=2,'space'=16] {'region','space'}, use_global_device_ids=true, to_apply=%region_3.4 | all-reduce | flops 1 | bytes 8 | tf_op jit(solution)/shard_map/psum | solution.py:87
  184.6 14.7 %scatter_custom_fusion.2 = f32[512]{0:T(512)S(1)} fusion(s32[2048]{0:T(1024)S(1)} %bitcast.157, f32[2048]{0:T(1024)S(1)} %mul.834, f32[]{:T(128)} %constant.32.clone.1), kind=kCustom, calls=%fused_computation.415 | custom fusion | flops 2048 | bytes 2052 | tf_op jit(solution)/shard_map/scatter-add | solution.py:166
  204.2 13.2 %gather_fusion = f32[2048]{0:T(1024)S(1)} fusion(f32[512]{0:T(512)S(1)} %bitcast.113, s32[2048]{0:T(1024)S(1)} %broadcast_clamp_fusion.1), kind=kCustom, calls=%fused_computation | custom fusion | bytes 24576 | tf_op jit(solution)/shard_map/gather | solution.py:172
  217.4 14.8 %scatter_custom_fusion.1 = f32[1024]{0:T(1024)S(1)} fusion(s32[2048]{0:T(1024)} %bitcast.158, f32[2048]{0:T(1024)S(1)} %mul.827, f32[]{:T(128)} %constant.32.clone.1), kind=kCustom, calls=%fused_computation.388 | custom fusion | flops 2048 | bytes 4608 | tf_op jit(solution)/shard_map/scatter-add | solution.py:171
  233.5 11.8 multiply_reduce_fusion.6
  246.5 41.9 %psum.64 = f32[]{:T(128)} all-reduce(f32[]{:T(128)S(6)} %add.765), channel_id=1, replica_groups=mesh['region'=2,'space'=16] {'region','space'}, use_global_device_ids=true, to_apply=%region_9.10 | all-reduce | flops 1 | bytes 8 | tf_op jit(solution)/shard_map/psum | solution.py:87
  367.4 12.7 %multiply_reduce_fusion.5 = (f32[]{:T(128)}, f32[1,8,128,128]{2,1,3,0:T(8,128)}) fusion(f32[1,8,128,128]{2,1,3,0:T(8,128)S(1)} %get-tuple-element.48, f32[1,10,130,130]{2,1,3,0:T(8,128)S(1)} %select_maximum_fusion.18, f32[1,8,128,128]{2,1,3,0:T(8,128)S(1)} %convert_multiply_fusion.9, f32[1,1,128,128]{2,1,3,0:T(1,128)S(1)} %collective-permute-done.13, ...), kind=kLoop, calls=%fused_computation.242 | loop fusion | flops 7602175 | bytes 5111876 | tf_op jit(solution)/shard_map/reduce_sum | solution.py:83
  381.4 46.1 %psum.65 = f32[]{:T(128)} all-reduce(f32[]{:T(128)S(6)} %add.792), channel_id=1, replica_groups=mesh['region'=2,'space'=16] {'region','space'}, use_global_device_ids=true, to_apply=%region_12.13 | all-reduce | flops 1 | bytes 8 | tf_op jit(solution)/shard_map/psum | solution.py:87
  444.9 14.8 %scatter_custom_fusion.4 = f32[512]{0:T(512)S(1)} fusion(s32[2048]{0:T(1024)} %bitcast.153, f32[2048]{0:T(1024)S(1)} %mul.876, f32[]{:T(128)} %constant.32.clone.1), kind=kCustom, calls=%fused_computation.413 | custom fusion | flops 2048 | bytes 2560 | tf_op jit(solution)/shard_map/scatter-add | solution.py:166
  465.3 13.2 %gather_fusion.2 = f32[2048]{0:T(1024)S(1)} fusion(f32[512]{0:T(512)S(1)} %bitcast.114, s32[2048]{0:T(1024)S(1)} %copy-done.8), kind=kCustom, calls=%fused_computation.2 | custom fusion | bytes 24576 | tf_op jit(solution)/shard_map/gather | solution.py:172
  478.5 14.8 %scatter_custom_fusion.3 = f32[1024]{0:T(1024)S(1)} fusion(s32[2048]{0:T(1024)} %bitcast.159, f32[2048]{0:T(1024)S(1)} %mul.869, f32[]{:T(128)} %constant.32.clone.1), kind=kCustom, calls=%fused_computation.386 | custom fusion | flops 2048 | bytes 4608 | tf_op jit(solution)/shard_map/scatter-add | solution.py:171
  494.6 12.6 %multiply_reduce_fusion.4 = (f32[]{:T(128)}, f32[1,8,128,128]{2,1,3,0:T(8,128)}) fusion(f32[1,8,128,128]{2,1,3,0:T(8,128)S(1)} %copy-done.1, f32[1,8,128,128]{2,1,3,0:T(8,128)S(1)} %copy.70, f32[]{:T(128)S(6)} %neg.28, f32[128]{0:T(128)S(1)} %copy-done.43, f32[8,128]{1,0:T(8,128)S(1)} %bitcast.145, f32[1,10,130,130]{2,1,3,0:T(8,128)S(1)} %select_maximum_fusion.16, ...), kind=kLoop, calls=%fused_computation.241 | loop fusion | flops 6946815 | bytes 5378632 | tf_op jit(solution)/shard_map/reduce_sum | solution.py:83
  508.4 40.8 %psum.66 = f32[]{:T(128)} all-reduce(f32[]{:T(128)S(6)} %add.803), channel_id=1, replica_groups=mesh['region'=2,'space'=16] {'region','space'}, use_global_device_ids=true, to_apply=%region_18.19 | all-reduce | flops 1 | bytes 8 | tf_op jit(solution)/shard_map/psum | solution.py:87
  549.9 11.6 convert_multiply_fusion.7
  629.3 12.7 %multiply_reduce_fusion.3 = (f32[]{:T(128)}, f32[1,8,128,128]{2,1,3,0:T(8,128)}) fusion(f32[1,8,128,128]{2,1,3,0:T(8,128)S(1)} %get-tuple-element.35, f32[1,10,130,130]{2,1,3,0:T(8,128)S(1)} %select_maximum_fusion.12, f32[1,8,128,128]{2,1,3,0:T(8,128)S(1)} %convert_multiply_fusion.6, f32[1,1,128,128]{2,1,3,0:T(1,128)S(1)} %collective-permute-done.21, ...), kind=kLoop, calls=%fused_computation.238 | loop fusion | flops 7602175 | bytes 5111876 | tf_op jit(solution)/shard_map/reduce_sum | solution.py:83
  643.3 45.9 %psum.67 = f32[]{:T(128)} all-reduce(f32[]{:T(128)S(6)} %add.830), channel_id=1, replica_groups=mesh['region'=2,'space'=16] {'region','space'}, use_global_device_ids=true, to_apply=%region_21.22 | all-reduce | flops 1 | bytes 8 | tf_op jit(solution)/shard_map/psum | solution.py:87
  707.1 14.8 %scatter_custom_fusion.6 = f32[512]{0:T(512)S(1)} fusion(s32[2048]{0:T(1024)} %bitcast.154, f32[2048]{0:T(1024)S(1)} %mul.926, f32[]{:T(128)} %constant.32.clone.1), kind=kCustom, calls=%fused_computation.411 | custom fusion | flops 2048 | bytes 2560 | tf_op jit(solution)/shard_map/scatter-add | solution.py:166
  727.5 13.2 %gather_fusion.4 = f32[2048]{0:T(1024)S(1)} fusion(f32[512]{0:T(512)S(1)} %bitcast.115, s32[2048]{0:T(1024)S(1)} %copy-done.9), kind=kCustom, calls=%fused_computation.4 | custom fusion | bytes 24576 | tf_op jit(solution)/shard_map/gather | solution.py:172
  740.7 14.8 %scatter_custom_fusion.5 = f32[1024]{0:T(1024)S(1)} fusion(s32[2048]{0:T(1024)} %bitcast.160, f32[2048]{0:T(1024)S(1)} %mul.919, f32[]{:T(128)} %constant.32.clone.1), kind=kCustom, calls=%fused_computation.384 | custom fusion | flops 2048 | bytes 4608 | tf_op jit(solution)/shard_map/scatter-add | solution.py:171
  756.7 12.6 %multiply_reduce_fusion.2 = (f32[]{:T(128)}, f32[1,8,128,128]{2,1,3,0:T(8,128)}) fusion(f32[1,8,128,128]{2,1,3,0:T(8,128)S(1)} %copy-done.4, f32[1,8,128,128]{2,1,3,0:T(8,128)S(1)} %get-tuple-element.48, f32[]{:T(128)S(6)} %neg.31, f32[128]{0:T(128)S(1)} %copy-done.44, f32[8,128]{1,0:T(8,128)S(1)} %bitcast.146, ...), kind=kLoop, calls=%fused_computation.237 | loop fusion | flops 6946815 | bytes 5378632 | tf_op jit(solution)/shard_map/reduce_sum | solution.py:83
  770.6 40.8 %psum.68 = f32[]{:T(128)} all-reduce(f32[]{:T(128)S(6)} %add.843), channel_id=1, replica_groups=mesh['region'=2,'space'=16] {'region','space'}, use_global_device_ids=true, to_apply=%region_27.28 | all-reduce | flops 1 | bytes 8 | tf_op jit(solution)/shard_map/psum | solution.py:87
  891.5 12.7 %multiply_reduce_fusion.1 = (f32[]{:T(128)}, f32[1,8,128,128]{2,1,3,0:T(8,128)}) fusion(f32[1,8,128,128]{2,1,3,0:T(8,128)S(1)} %get-tuple-element.22, f32[1,10,130,130]{2,1,3,0:T(8,128)S(1)} %select_maximum_fusion.6, f32[1,8,128,128]{2,1,3,0:T(8,128)S(1)} %convert_multiply_fusion.3, f32[1,1,128,128]{2,1,3,0:T(1,128)S(1)} %collective-permute-done.29, ...), kind=kLoop, calls=%fused_computation.234 | loop fusion | flops 7602175 | bytes 5111876 | tf_op jit(solution)/shard_map/reduce_sum | solution.py:83
  905.5 45.7 %psum.69 = f32[]{:T(128)} all-reduce(f32[]{:T(128)S(6)} %add.870), channel_id=1, replica_groups=mesh['region'=2,'space'=16] {'region','space'}, use_global_device_ids=true, to_apply=%region_30.31 | all-reduce | flops 1 | bytes 8 | tf_op jit(solution)/shard_map/psum | solution.py:87
  970.2 14.8 %scatter_custom_fusion.8 = f32[512]{0:T(512)S(1)} fusion(s32[2048]{0:T(1024)} %bitcast.155, f32[2048]{0:T(1024)S(1)} %mul.978, f32[]{:T(128)} %constant.32.clone.1), kind=kCustom, calls=%fused_computation.409 | custom fusion | flops 2048 | bytes 2560 | tf_op jit(solution)/shard_map/scatter-add | solution.py:166
  990.5 13.2 %gather_fusion.6 = f32[2048]{0:T(1024)S(1)} fusion(f32[512]{0:T(512)S(1)} %bitcast.112, s32[2048]{0:T(1024)S(1)} %copy-done.10), kind=kCustom, calls=%fused_computation.6 | custom fusion | bytes 24576 | tf_op jit(solution)/shard_map/gather | solution.py:172
  1003.8 14.8 %scatter_custom_fusion.7 = f32[1024]{0:T(1024)S(1)} fusion(s32[2048]{0:T(1024)} %bitcast.161, f32[2048]{0:T(1024)S(1)} %mul.971, f32[]{:T(128)} %constant.32.clone.1), kind=kCustom, calls=%fused_computation.382 | custom fusion | flops 2048 | bytes 4608 | tf_op jit(solution)/shard_map/scatter-add | solution.py:171
  1019.8 13.6 %multiply_reduce_fusion = (f32[]{:T(128)}, f32[1,8,128,128]{2,1,3,0:T(8,128)}) fusion(f32[1,8,128,128]{2,1,3,0:T(8,128)} %get-tuple-element.16, f32[1,8,128,128]{2,1,3,0:T(8,128)S(1)} %get-tuple-element.35, f32[]{:T(128)S(6)} %neg.34, f32[128]{0:T(128)S(1)} %copy-done.45, f32[8,128]{1,0:T(8,128)S(1)} %bitcast.144, ...), kind=kLoop, calls=%fused_computation.233 | loop fusion | flops 6946815 | bytes 5378632 | tf_op jit(solution)/shard_map/reduce_sum | solution.py:83
  1034.7 41.8 %psum.70 = f32[]{:T(128)} all-reduce(f32[]{:T(128)S(6)} %add.883), channel_id=1, replica_groups=mesh['region'=2,'space'=16] {'region','space'}, use_global_device_ids=true, to_apply=%region_36.37 | all-reduce | flops 1 | bytes 8 | tf_op jit(solution)/shard_map/psum | solution.py:87
  1156.9 11.9 fusion.92
  1170.1 45.1 %psum.71 = f32[]{:T(128)} all-reduce(f32[]{:T(128)S(6)} %add.910), channel_id=1, replica_groups=mesh['region'=2,'space'=16] {'region','space'}, use_global_device_ids=true, to_apply=%region_39.40 | all-reduce | flops 1 | bytes 8 | tf_op jit(solution)/shard_map/psum | solution.py:87
  (358 shorter events, 486.9 us)
Async XLA Ops:
  16.1 35.3 %collective-permute-start = (f32[1,1,128,128]{2,1,3,0:T(1,128)S(1)}, f32[1,1,128,128]{2,1,3,0:T(1,128)S(1)}, u32[]{:S(2)}, u32[]{:S(2)}) collective-permute-start(f32[1,1,128,128]{2,1,3,0:T(1,128)S(1)} %get-tuple-element.92), channel_id=1, source_target_pairs={{1,0},{2,1},{3,2},{4,3},{5,4},{6,5},{7,6},{8,7},{9,8},{10,9},{11,1... | collective-permute-start | bytes 196616 | tf_op jit(solution)/shard_map/ppermute | solution.py:22
  17.4 34.0 %collective-permute-start.1 = (f32[1,1,128,128]{2,1,3,0:T(1,128)S(1)}, f32[1,1,128,128]{2,1,3,0:T(1,128)S(1)}, u32[]{:S(2)}, u32[]{:S(2)}) collective-permute-start(f32[1,1,128,128]{2,1,3,0:T(1,128)S(1)} %get-tuple-element.91), channel_id=1, source_target_pairs={{0,1},{1,2},{2,3},{3,4},{4,5},{5,6},{6,7},{7,8},{8,9},{9,10},{10,1... | collective-permute-start | bytes 196616 | tf_op jit(solution)/shard_map/ppermute | solution.py:21
  76.8 8.2 collective-permute-start.2
  78.1 7.0 collective-permute-start.3
  96.9 7.1 collective-permute-start.4
  98.2 7.3 collective-permute-start.5
  169.9 62.4 %collective-permute-start.6 = (f32[1,1,128,128]{2,1,3,0:T(1,128)S(1)}, f32[1,1,128,128]{2,1,3,0:T(1,128)S(1)}, u32[]{:S(2)}, u32[]{:S(2)}) collective-permute-start(f32[1,1,128,128]{2,1,3,0:T(1,128)S(1)} %get-tuple-element.88), channel_id=1, source_target_pairs={{1,0},{2,1},{3,2},{4,3},{5,4},{6,5},{7,6},{8,7},{9,8},{10,9},{11,1... | collective-permute-start | bytes 196616 | tf_op jit(solution)/shard_map/ppermute | solution.py:22
  171.2 61.1 %collective-permute-start.7 = (f32[1,1,128,128]{2,1,3,0:T(1,128)S(1)}, f32[1,1,128,128]{2,1,3,0:T(1,128)S(1)}, u32[]{:S(2)}, u32[]{:S(2)}) collective-permute-start(f32[1,1,128,128]{2,1,3,0:T(1,128)S(1)} %get-tuple-element.87), channel_id=1, source_target_pairs={{0,1},{1,2},{2,3},{3,4},{4,5},{5,6},{6,7},{7,8},{8,9},{9,10},{10,1... | collective-permute-start | bytes 196616 | tf_op jit(solution)/shard_map/ppermute | solution.py:21
  335.3 6.8 collective-permute-start.10
  336.6 7.0 collective-permute-start.11
  357.3 8.0 collective-permute-start.12
  358.6 7.7 collective-permute-start.13
  430.2 63.2 %collective-permute-start.14 = (f32[1,1,128,128]{2,1,3,0:T(1,128)}, f32[1,1,128,128]{2,1,3,0:T(1,128)S(1)}, u32[]{:S(2)}, u32[]{:S(2)}) collective-permute-start(f32[1,1,128,128]{2,1,3,0:T(1,128)} %get-tuple-element.82), channel_id=1, source_target_pairs={{1,0},{2,1},{3,2},{4,3},{5,4},{6,5},{7,6},{8,7},{9,8},{10,9},{11,1... | collective-permute-start | bytes 196616 | tf_op jit(solution)/shard_map/ppermute | solution.py:22
  431.5 61.9 %collective-permute-start.15 = (f32[1,1,128,128]{2,1,3,0:T(1,128)S(1)}, f32[1,1,128,128]{2,1,3,0:T(1,128)S(1)}, u32[]{:S(2)}, u32[]{:S(2)}) collective-permute-start(f32[1,1,128,128]{2,1,3,0:T(1,128)S(1)} %get-tuple-element.81), channel_id=1, source_target_pairs={{0,1},{1,2},{2,3},{3,4},{4,5},{5,6},{6,7},{7,8},{8,9},{9,10},{10,1... | collective-permute-start | bytes 196616 | tf_op jit(solution)/shard_map/ppermute | solution.py:21
  563.0 6.7 collective-permute-start.17
  597.2 6.8 collective-permute-start.18
  598.5 7.0 collective-permute-start.19
  619.2 7.8 collective-permute-start.20
  620.5 7.7 collective-permute-start.21
  692.0 63.6 %collective-permute-start.22 = (f32[1,1,128,128]{2,1,3,0:T(1,128)}, f32[1,1,128,128]{2,1,3,0:T(1,128)S(1)}, u32[]{:S(2)}, u32[]{:S(2)}) collective-permute-start(f32[1,1,128,128]{2,1,3,0:T(1,128)} %get-tuple-element.76), channel_id=1, source_target_pairs={{1,0},{2,1},{3,2},{4,3},{5,4},{6,5},{7,6},{8,7},{9,8},{10,9},{11,1... | collective-permute-start | bytes 196616 | tf_op jit(solution)/shard_map/ppermute | solution.py:22
  693.2 62.3 %collective-permute-start.23 = (f32[1,1,128,128]{2,1,3,0:T(1,128)S(1)}, f32[1,1,128,128]{2,1,3,0:T(1,128)S(1)}, u32[]{:S(2)}, u32[]{:S(2)}) collective-permute-start(f32[1,1,128,128]{2,1,3,0:T(1,128)S(1)} %get-tuple-element.75), channel_id=1, source_target_pairs={{0,1},{1,2},{2,3},{3,4},{4,5},{5,6},{6,7},{7,8},{8,9},{9,10},{10,1... | collective-permute-start | bytes 196616 | tf_op jit(solution)/shard_map/ppermute | solution.py:21
  825.2 6.7 collective-permute-start.25
  859.4 6.8 collective-permute-start.26
  860.7 7.0 collective-permute-start.27
  881.4 8.0 collective-permute-start.28
  882.7 7.7 collective-permute-start.29
  954.6 64.0 %collective-permute-start.30 = (f32[1,1,128,128]{2,1,3,0:T(1,128)}, f32[1,1,128,128]{2,1,3,0:T(1,128)S(1)}, u32[]{:S(2)}, u32[]{:S(2)}) collective-permute-start(f32[1,1,128,128]{2,1,3,0:T(1,128)} %get-tuple-element.70), channel_id=1, source_target_pairs={{1,0},{2,1},{3,2},{4,3},{5,4},{6,5},{7,6},{8,7},{9,8},{10,9},{11,1... | collective-permute-start | bytes 196616 | tf_op jit(solution)/shard_map/ppermute | solution.py:22
  955.8 62.8 %collective-permute-start.31 = (f32[1,1,128,128]{2,1,3,0:T(1,128)S(1)}, f32[1,1,128,128]{2,1,3,0:T(1,128)S(1)}, u32[]{:S(2)}, u32[]{:S(2)}) collective-permute-start(f32[1,1,128,128]{2,1,3,0:T(1,128)S(1)} %get-tuple-element.69), channel_id=1, source_target_pairs={{0,1},{1,2},{2,3},{3,4},{4,5},{5,6},{6,7},{7,8},{8,9},{9,10},{10,1... | collective-permute-start | bytes 196616 | tf_op jit(solution)/shard_map/ppermute | solution.py:21
  1122.3 12.5 %collective-permute-start.34 = (f32[1,1,64,64]{2,1,3,0:T(1,128)S(1)}, f32[1,1,64,64]{2,1,3,0:T(1,128)S(1)}, u32[]{:S(2)}, u32[]{:S(2)}) collective-permute-start(f32[1,1,64,64]{2,1,3,0:T(1,128)S(1)} %get-tuple-element.94), channel_id=1, source_target_pairs={{1,0},{2,1},{3,2},{4,3},{5,4},{6,5},{7,6},{8,7},{9,8},{10,9},{11,1... | collective-permute-start | bytes 49160 | tf_op jit(solution)/shard_map/ppermute | solution.py:22
  1123.6 11.2 collective-permute-start.35
  1146.7 8.0 collective-permute-start.36
  1148.0 7.7 collective-permute-start.37
  (57 other events, 2074.7 us)
where the time goes:
time: 1230 us; the launch traced here: 1220 us
  other arithmetic  450 us (37%)
  blocking collectives  412 us (33%)
  local copies, waits for them, and re-layouts  186 us (15%)
  starting transfers between devices  126 us (10%)
  between operations  27.4 us (2%)
  waiting for transfers between devices  18.5 us (2%)
    psum x9, blocking collectives, global_inner(): return lax.psum(local_inner(first, second), ('region', 'space'))  395 us
    reduce_sum x18, other arithmetic, local_inner(): return jnp.sum(first[0] * second[0]) + jnp.sum(first[1] * second[1])  121 us
    mul x13, other arithmetic, fine_apply(): active * cells  104 us
    ppermute x19, starting transfers between devices, padded_2(): before = lax.ppermute(last, axis, up)  101 us
    slice x12, local copies, waits for them, and re-layouts, coarsen(): values = values[:, :, 0::2] + values[:, :, 1::2]  67.8 us
    scatter-add x4, other arithmetic, on_device(): jax.ops.segment_sum(side_sign * margin_coef * paired[mort_list], own_list...  59.3 us
    scatter-add x4, other arithmetic, on_device(): jax.ops.segment_sum(side_sign * margin_coef * face_cells[own_list], mort_...  59.1 us
    sub x5, other arithmetic, vcycle(): coarse_rhs = coarsen(resid - first_image)  55.7 us
  transfers between devices with their start and end apart: 38, of which 20 were waited for; matrix products, arithmetic and copies ran while one was open for 20% of the time, Pallas kernels for 0%

commit v1 on v0

v1 whole, which is shorter than its diff:
```python
import functools

import jax
import jax.numpy as jnp
from jax import lax
from jax.experimental import pallas as pl
from jax.experimental.pallas import tpu as pltpu
from jax.sharding import PartitionSpec as P

ZONES = 16
ITERS = 4
OMEGA = 0.8
STAB = 0.05
F32 = jnp.float32
BF16 = jnp.bfloat16
MESH = pl.DeviceIdType.MESH


def radices(count):
    found = []
    while count > 1:
        step = 4 if count % 4 == 0 else (2 if count % 2 == 0 else count)
        found.append(step)
        count //= step
    return found or [1]


def kernel(
    regions,
    spaces,
    f_ref,
    g_ref,
    mask_ref,
    zone_ref,
    zcoef_ref,
    mort_ref,
    stokes_ref,
    darcy_ref,
    weight_ref,
    tiles_ref,
    x_ref,
    xm_ref,
    ar,
    act,
    diag,
    inv,
    ay,
    q,
    ae,
    ys,
    rs,
    icoarse,
    s1,
    spack,
    srecv,
    tmp,
    meta,
    metax,
    mx,
    lamx,
    lams,
    part,
    prow,
    acc,
    red,
    halo_send,
    halo_recv,
    lam_send,
    lam_recv,
    part_sem,
    red_send,
    red_recv,
):
    reg = lax.axis_index("region")
    pos = lax.axis_index("space")
    slab = f_ref.shape[1]
    ny, nz = f_ref.shape[2], f_ref.shape[3]
    nc = slab // 2
    hy = ny // 2
    mort = g_ref.shape[1]
    rows = mort_ref.shape[1]
    has_left = pos > 0
    has_right = pos < spaces - 1
    sides = ((-1, has_left), (1, has_right))
    first_region = reg == 0

    lane = lax.broadcasted_iota(jnp.int32, (ny, nz), 1)
    row = lax.broadcasted_iota(jnp.int32, (ny, nz), 0)
    layer_lane = reg * (nz - 1)
    clane = lax.broadcasted_iota(jnp.int32, (hy, nz), 1)
    crow = lax.broadcasted_iota(jnp.int32, (hy, nz), 0)
    ceven = clane % 2 == 0

    stages = []
    stride = 1
    for number, radix in enumerate(radices(spaces)):
        digit = (pos // stride) % radix
        base = pos - digit * stride
        peers = []
        for d_reg in range(regions if number == 0 else 1):
            for j in range(radix):
                if d_reg == 0 and j == 0:
                    continue
                peers.append((
                    d_reg * radix + j,
                    ((reg + d_reg) % regions, base + ((digit + j) % radix) * stride),
                ))
        stages.append(peers)
        stride *= radix

    barrier = pltpu.get_barrier_semaphore()
    waits = 0
    for peers in stages:
        for _, who in peers:
            pl.semaphore_signal(barrier, inc=1, device_id=who, device_id_type=MESH)
            waits += 1
    for step, there in sides:
        for d_reg in range(regions):
            @pl.when(there)
            def _():
                pl.semaphore_signal(
                    barrier, inc=1, device_id=((reg + d_reg) % regions, pos + step),
                    device_id_type=MESH,
                )
    beside = has_left.astype(jnp.int32) + has_right.astype(jnp.int32)
    pl.semaphore_wait(barrier, waits + regions * beside)

    def halo(kind, step, src, dst):
        side = (step + 1) // 2
        return pltpu.make_async_remote_copy(
            src_ref=src, dst_ref=dst,
            send_sem=halo_send.at[kind, side], recv_sem=halo_recv.at[kind, 1 - side],
            device_id=(reg, pos + step), device_id_type=MESH,
        )

    def start_halo(kind, src_of, dst_of):
        for step, there in sides:
            @pl.when(there)
            def _():
                halo(kind, step, src_of(step), dst_of(step)).start()

    def wait_halo(kind, src_of, dst_of):
        for step, there in sides:
            @pl.when(there)
            def _():
                halo(kind, step, src_of(step), dst_of(step)).wait_send()
                pltpu.make_async_remote_copy(
                    src_ref=src_of(-step), dst_ref=dst_of(-step),
                    send_sem=halo_send.at[kind, (1 - step) // 2],
                    recv_sem=halo_recv.at[kind, (step + 1) // 2],
                    device_id=(reg, pos + step), device_id_type=MESH,
                ).wait_recv()

    zero = jnp.zeros((ny, nz), F32)

    def clear(side_lo, there):
        @pl.when(jnp.logical_not(there))
        def _():
            for d in range(2):
                at = side_lo * (slab + 2) + d
                ar[at] = zero
                for k in range(ITERS):
                    ys[k, at] = zero
                srecv[side_lo] = jnp.zeros((hy, nz), F32)
            q[side_lo * (slab + 1)] = zero
            for k in range(3):
                metax[side_lo, k] = jnp.zeros((1, rows), F32)
            for d_reg in range(regions):
                lamx[2 * side_lo, d_reg] = jnp.zeros((1, mort), F32)

    f_src = lambda step: f_ref.at[0, pl.ds(0 if step < 0 else slab - 1, 1)]
    f_dst = lambda step: q.at[pl.ds(slab + 1 if step < 0 else 0, 1)]
    ar_src = lambda step: ar.at[pl.ds(2 if step < 0 else slab, 2)]
    ar_dst = lambda step: ar.at[pl.ds(slab + 2 if step < 0 else 0, 2)]
    meta_src = lambda step: meta
    meta_dst = lambda step: metax.at[1 if step < 0 else 0]

    def y_src(k):
        return lambda step: ys.at[k, pl.ds(2 if step < 0 else slab, 2)]

    def y_dst(k):
        return lambda step: ys.at[k, pl.ds(slab + 2 if step < 0 else 0, 2)]

    s_src = lambda step: spack.at[0 if step < 0 else 1]
    s_dst = lambda step: srecv.at[1 if step < 0 else 0]

    def react_layer(l):
        ids = zone_ref[0, l]
        value = jnp.zeros((ny, nz), F32)
        for zone in range(ZONES):
            value = jnp.where(ids == zone, zcoef_ref[zone], value)
        ar[l + 2] = jnp.where(mask_ref[0, l] != 0, value, 0.0)

    @pl.loop(0, slab)
    def _(l):
        react_layer(l)

    start_halo(1, ar_src, ar_dst)
    clear(0, has_left)
    clear(1, has_right)

    lane_row = lax.broadcasted_iota(jnp.int32, (1, rows), 1)
    limit = jnp.zeros((1, rows), jnp.int32)
    for tile in range(rows // 128):
        limit = jnp.where(lane_row // 128 == tile, tiles_ref[0, tile], limit)
    coef = jnp.where(lane_row % 128 < limit, weight_ref[...], 0.0)
    side_sign = jnp.where(first_region, 1.0, -1.0).astype(F32)
    meta[0] = mort_ref[...].astype(F32)
    meta[1] = jnp.where(first_region, stokes_ref[...], darcy_ref[...]).astype(F32)
    meta[2] = coef * side_sign
    start_halo(2, meta_src, meta_dst)
    start_halo(0, f_src, f_dst)

    @pl.loop(0, slab)
    def _(l):
        q[l + 1] = f_ref[0, l]
        rs[0, l] = f_ref[0, l]

    width = 256

    def split(value):
        high = value.astype(BF16).astype(F32)
        rest = value - high
        mid = rest.astype(BF16).astype(F32)
        return high, mid, rest - mid

    def nt_dot(a, b):
        return lax.dot_general(a, b, (((1,), (1,)), ((), ())), preferred_element_type=F32)

    multiplier = lax.broadcasted_iota(jnp.int32, (2 * mort, width), 0).astype(F32)

    def add_pairs(source, first_layer, layers, target, squares):
        face = lax.broadcasted_iota(jnp.int32, (ny, width), 0).astype(F32)
        total = jnp.zeros((8, 2 * mort), F32)
        for chunk in range(rows // width):
            span = pl.ds(chunk * width, width)
            mort_row, face_row, coef_row = (source[k, :, span] for k in range(3))
            one_hot = jnp.where(multiplier == mort_row, 1.0, 0.0).astype(BF16)
            pieces = split(coef_row)

            def body(l, carry):
                hit = face == face_row - ((first_layer + l) * ny).astype(F32)
                at = pl.ds(pl.multiple_of((target + l) * ny, ny), ny)
                value = jnp.zeros((ny, 2 * mort), F32)
                for piece in pieces:
                    value = value + nt_dot(jnp.where(hit, piece, 0.0).astype(BF16), one_hot)
                if chunk == 0:
                    mx[at, :] = value
                else:
                    mx[at, :] = mx[at, :] + value
                return carry

            lax.fori_loop(0, layers, body, 0)
            if squares:
                for piece in split(coef_row * coef_row):
                    total = total + nt_dot(
                        jnp.broadcast_to(piece, (8, width)).astype(BF16), one_hot
                    )
        return total[0:1]

    squares = add_pairs(meta, 0, slab, 1, True)
    own_half = lambda v: jnp.where(first_region, v[:, :mort], v[:, mort:])
    other_half = lambda v: jnp.where(first_region, v[:, mort:], v[:, :mort])
    inv_mort = 1.0 / (STAB + own_half(squares) / 3.0)

    wait_halo(2, meta_src, meta_dst)
    add_pairs(metax.at[0], slab - 1, 1, 0, False)
    add_pairs(metax.at[1], 0, 1, slab + 1, False)
    wait_halo(1, ar_src, ar_dst)

    @pl.loop(0, slab + 4)
    def _(l):
        act[l] = jnp.where(ar[l] > 0.0, 1.0, 0.0)

    @pl.loop(0, slab + 2)
    def _(l):
        value = jnp.where(ar[l + 1] > 0.0, 6.0 + ar[l + 1], 1.0)
        diag[l] = value
        inv[l] = OMEGA / value

    def pair_sum(total):
        tmp[...] = total
        v = tmp[pl.ds(0, hy, stride=2), :] + tmp[pl.ds(1, hy, stride=2), :]
        return v + jnp.where(ceven, pltpu.roll(v, nz - 1, 1), pltpu.roll(v, 1, 1))

    @pl.loop(0, nc + 2)
    def _(b):
        icoarse[b] = OMEGA / (12.0 + 0.25 * pair_sum(ar[2 * b] + ar[2 * b + 1]))

    def in_layer(c):
        total = jnp.where(row == 0, 0.0, pltpu.roll(c, 1, 0))
        total = total + jnp.where(row == ny - 1, 0.0, pltpu.roll(c, ny - 1, 0))
        total = total + jnp.where(lane == 0, 0.0, pltpu.roll(c, 1, 1))
        return total + jnp.where(lane == nz - 1, 0.0, pltpu.roll(c, nz - 1, 1))

    def neighbours(ref, at):
        return in_layer(ref[at]) + (ref[at - 1] + ref[at + 1])

    def coarse_in_layer(c):
        total = jnp.where(crow == 0, 0.0, pltpu.roll(c, 1, 0))
        total = total + jnp.where(crow == hy - 1, 0.0, pltpu.roll(c, hy - 1, 0))
        total = total + jnp.where(clane < 2, 0.0, pltpu.roll(c, 2, 1))
        return total + jnp.where(clane >= nz - 2, 0.0, pltpu.roll(c, nz - 2, 1))

    def scale_first(l):
        ae[l] = act[l + 1] * (inv[l] * q[l])

    def coarse_first(b):
        total = jnp.zeros((ny, nz), F32)
        for d in range(2):
            l = 2 * b + d + 1
            total = total + (0.2 * q[l] + act[l + 1] * neighbours(ae, l))
        s1[b + 2] = icoarse[b + 1] * pair_sum(total)

    def send_coarse():
        spack[0] = jnp.where(ceven, s1[2], s1[3])
        spack[1] = jnp.where(ceven, s1[nc], s1[nc + 1])
        start_halo(3, s_src, s_dst)

    def receive_coarse():
        wait_halo(3, s_src, s_dst)
        for side, at in ((0, 0), (1, nc + 2)):
            v = srecv[side]
            s1[at] = jnp.where(ceven, v, pltpu.roll(v, 1, 1))
            s1[at + 1] = jnp.where(ceven, pltpu.roll(v, nz - 1, 1), v)

    def second_block(b):
        s2 = 1.2 * s1[b + 1] + 2.0 * icoarse[b] * (
            coarse_in_layer(s1[b + 1]) + (s1[b] + s1[b + 2])
        )
        tmp[pl.ds(0, hy, stride=2), :] = s2
        tmp[pl.ds(1, hy, stride=2), :] = s2
        return tmp[...]

    e2 = ay

    def second_all():
        up = second_block(0)
        e2[0] = inv[0] * q[0] + up
        ae[0] = act[1] * e2[0]
        up = second_block(nc + 1)
        e2[slab + 1] = inv[slab + 1] * q[slab + 1] + up
        ae[slab + 1] = act[slab + 2] * e2[slab + 1]

        @pl.loop(1, nc + 1)
        def _(b):
            up = second_block(b)
            for d in range(2):
                l = 2 * b - 1 + d
                value = inv[l] * q[l] + up
                e2[l] = value
                ae[l] = act[l + 1] * value

    def last_layer(l):
        return 0.2 * e2[l] + inv[l] * (q[l] + act[l + 1] * neighbours(ae, l))

    def fold(v):
        out = v[:, 0:128]
        for k in range(1, v.shape[1] // 128):
            out = out + v[:, 128 * k : 128 * (k + 1)]
        return out

    def lay_sum(v):
        return jnp.sum(v.reshape(ny // 8, 8, nz), axis=0)

    def red_copy(parity, number, slot, who):
        return pltpu.make_async_remote_copy(
            src_ref=acc.at[parity, number], dst_ref=red.at[parity, number, slot],
            send_sem=red_send.at[parity, number, slot],
            recv_sem=red_recv.at[parity, number, slot],
            device_id=who, device_id_type=MESH,
        )

    def red_start(parity, number):
        for slot, who in stages[number]:
            red_copy(parity, number, slot, who).start()

    def red_wait(parity, number):
        for slot, who in stages[number]:
            red_copy(parity, number, slot, who).wait()
        total = acc[parity, number]
        for slot, _ in stages[number]:
            total = total + red[parity, number, slot]
        return total

    def red_next(parity, number):
        acc[parity, number + 1] = red_wait(parity, number)
        red_start(parity, number + 1)

    last_stage = len(stages) - 1

    def lam_copy(k, step, d_reg, sending):
        there = step if sending else -step
        return pltpu.make_async_remote_copy(
            src_ref=lams.at[k], dst_ref=lamx.at[1 - there, d_reg],
            send_sem=lam_send.at[there + 1, d_reg], recv_sem=lam_recv.at[1 - there, d_reg],
            device_id=((reg + d_reg) % regions, pos + step), device_id_type=MESH,
        )

    def lam_each(action):
        for step, there in ((-1, has_left), (0, None), (1, has_right)):
            for d_reg in range(regions):
                if step == 0:
                    if d_reg:
                        action(step, d_reg)
                else:
                    pl.when(there)(functools.partial(action, step, d_reg))

    def lam_start(k):
        lam_each(lambda step, d_reg: lam_copy(k, step, d_reg, True).start())

    def lam_wait(k):
        def both(step, d_reg):
            lam_copy(k, step, d_reg, True).wait_send()
            lam_copy(k, step, d_reg, False).wait_recv()

        lam_each(both)

    def paired(offset, own):
        mine, others = own, lamx[offset, 1]
        return jnp.concatenate(
            [jnp.where(first_region, mine, others), jnp.where(first_region, others, mine)], axis=1
        )

    def apply_cells(k, l):
        y = ys[k, l + 1]
        q[l] = diag[l] * y - act[l + 1] * neighbours(ay, l + 1)

    def add_face(l, lam_row):
        at = pl.ds(l * ny if isinstance(l, int) else pl.multiple_of(l * ny, ny), ny)
        col = jnp.sum(mx[at, :] * lam_row, axis=1, keepdims=True)
        q[l] = q[l] + jnp.where(lane == layer_lane, col, 0.0)

    wait_halo(0, f_src, f_dst)

    @pl.loop(0, slab + 2)
    def _(l):
        scale_first(l)

    @pl.loop(0, nc)
    def _(b):
        coarse_first(b)

    send_coarse()
    res_m = [g_ref[...]]
    lam = g_ref[...] * inv_mort
    lams[0] = lam
    lam_start(0)
    receive_coarse()
    second_all()

    one = jnp.ones((1, 1), F32)
    mults = [lam]
    beta_prev = None
    ry_local = None
    coefs_old, coefs_new, coefs_x = [], [], []
    cosine, sine = -one, 0.0 * one
    delta_bar, epsilon = 0.0 * one, 0.0 * one
    phi_bar = None

    def out_pass(k, scales):
        def body(l, total):
            value = last_layer(l + 1)
            if scales is None:
                resid = rs[0, l]
            else:
                s_q, s_old, s_now = scales
                value = s_q * value - s_now * ys[k - 1, l + 2]
                resid = s_q * q[l + 1] - s_now * rs[(k - 1) % 3, l]
                if s_old is not None:
                    value = value - s_old * ys[k - 2, l + 2]
                    resid = resid - s_old * rs[(k - 2) % 3, l]
                rs[k % 3, l] = resid
            ys[k, l + 2] = value
            return total + lay_sum(value * resid)

        total = jnp.zeros((8, nz), F32)
        total = lax.fori_loop(0, 2, body, total)
        total = lax.fori_loop(slab - 2, slab, body, total)
        if k < ITERS:
            start_halo(4, y_src(k), y_dst(k))
        total = lax.fori_loop(2, slab - 2, body, total)
        return jnp.sum(total, axis=0, keepdims=True)

    ry_local = out_pass(0, None) + fold(lam * res_m[0])
    for k in range(ITERS):
        parity = k % 2
        lam = mults[k]

        @pl.loop(2, slab + 2)
        def _(l):
            ay[l] = act[l] * ys[k, l]

        lam_wait(k)
        own_pair = paired(1, lam)

        def operate(l, carry):
            apply_cells(k, l)
            add_face(l, own_pair)
            y = ys[k, l + 1]
            u = jnp.where(first_region, y[:, 0:1], y[:, nz - 1 : nz])
            at = pl.ds(pl.multiple_of(l * ny, ny), ny)
            prod, old, prt = carry
            prod = prod + lay_sum(y * q[l])
            if k > 0:
                old = old + lay_sum(y * rs[(k - 1) % 3, l - 1])
            prt = prt + jnp.sum((mx[at, :] * u).reshape(ny // 8, 8, 2 * mort), axis=0)
            scale_first(l)
            return prod, old, prt

        carry = (
            jnp.zeros((8, nz), F32),
            jnp.zeros((8, nz), F32),
            jnp.zeros((8, 2 * mort), F32),
        )
        carry = lax.fori_loop(2, slab, operate, carry)

        @pl.loop(1, nc - 1)
        def _(b):
            coarse_first(b)

        wait_halo(4, y_src(k), y_dst(k))
        for l in (0, 1, slab + 2, slab + 3):
            ay[l] = act[l] * ys[k, l]
        carry = operate(jnp.int32(1), carry)
        prod, old, prt = operate(jnp.int32(slab), carry)
        apply_cells(k, 0)
        apply_cells(k, slab + 1)
        add_face(0, paired(0, lamx[0, 0]))
        add_face(slab + 1, paired(2, lamx[2, 0]))
        scale_first(0)
        scale_first(slab + 1)
        coarse_first(0)
        coarse_first(nc - 1)
        send_coarse()
        partial_rows = jnp.sum(prt, axis=0, keepdims=True)
        prow[...] = other_half(partial_rows)
        part_copy = pltpu.make_async_remote_copy(
            src_ref=prow, dst_ref=part, send_sem=part_sem.at[0], recv_sem=part_sem.at[1],
            device_id=((reg + 1) % regions, pos), device_id_type=MESH,
        )
        part_copy.start()
        prod_row = jnp.sum(prod, axis=0, keepdims=True)
        prod_row = prod_row + fold(own_pair * partial_rows) - STAB * fold(lam * lam)
        old_row = jnp.sum(old, axis=0, keepdims=True)
        if k > 0:
            old_row = old_row + fold(lam * res_m[k - 1])
        acc[parity, 0, 0:1] = ry_local
        acc[parity, 0, 1:2] = prod_row
        acc[parity, 0, 2:3] = old_row
        acc[parity, 0, 3:8] = jnp.zeros((5, 128), F32)
        red_start(parity, 0)
        receive_coarse()
        for number in range(last_stage):
            red_next(parity, number)
        part_copy.wait()
        q_m = own_half(partial_rows) + part[...] - STAB * lam
        second_all()
        total = red_wait(parity, last_stage)
        sums = jnp.sum(total, axis=1, keepdims=True)
        ry, yky, yr = sums[0:1], sums[1:2], sums[2:3]
        beta = jnp.sqrt(ry)
        alpha = yky / ry
        if k > 0:
            alpha = alpha - yr / beta_prev
        def rotate(alpha_now, beta_next, column):
            nonlocal cosine, sine, delta_bar, epsilon, phi_bar
            nonlocal coefs_old, coefs_new, coefs_x
            old_eps = epsilon
            delta = cosine * delta_bar + sine * alpha_now
            gamma_bar = sine * delta_bar - cosine * alpha_now
            epsilon = sine * beta_next
            delta_bar = -cosine * beta_next
            gamma = jnp.sqrt(gamma_bar * gamma_bar + beta_next * beta_next)
            cosine = gamma_bar / gamma
            sine = beta_next / gamma
            phi = cosine * phi_bar
            phi_bar = sine * phi_bar
            now = []
            for i in range(column + 1):
                value = 1.0 / betas[i] if i == column else 0.0 * one
                if i < len(coefs_old):
                    value = value - old_eps * coefs_old[i]
                if i < len(coefs_new):
                    value = value - delta * coefs_new[i]
                now.append(value / gamma)
            coefs_old, coefs_new = coefs_new, now
            coefs_x = [
                (coefs_x[i] if i < len(coefs_x) else 0.0) + phi * now[i]
                for i in range(column + 1)
            ]

        if k == 0:
            phi_bar = beta
            betas = [beta]
        else:
            betas.append(beta)
            rotate(alpha_prev, beta, k - 1)
        scales = (1.0 / beta, None if k == 0 else beta / beta_prev, alpha / beta)
        next_res = scales[0] * q_m - scales[2] * res_m[k]
        next_lam = scales[0] * (q_m * inv_mort) - scales[2] * lam
        if k > 0:
            next_res = next_res - scales[1] * res_m[k - 1]
            next_lam = next_lam - scales[1] * mults[k - 1]
        res_m.append(next_res)
        mults.append(next_lam)
        if k + 1 < ITERS:
            lams[k + 1] = next_lam
            lam_start(k + 1)
        ry_local = out_pass(k + 1, scales) + fold(next_lam * next_res)
        beta_prev, alpha_prev = beta, alpha

    parity = ITERS % 2
    acc[parity, 0, 0:1] = ry_local
    acc[parity, 0, 1:8] = jnp.zeros((7, 128), F32)
    red_start(parity, 0)
    for number in range(last_stage):
        red_next(parity, number)
    total = red_wait(parity, last_stage)
    rotate(alpha_prev, jnp.sqrt(jnp.sum(total[0:1], axis=1, keepdims=True)), ITERS - 1)

    @pl.loop(0, slab)
    def _(l):
        value = coefs_x[0] * ys[0, l + 2]
        for k in range(1, ITERS):
            value = value + coefs_x[k] * ys[k, l + 2]
        x_ref[0, l] = value

    value = coefs_x[0] * mults[0]
    for k in range(1, ITERS):
        value = value + coefs_x[k] * mults[k]
    xm_ref[...] = value


def on_device(regions, spaces, *args):
    f_cells, g_mortar, rows = args[0], args[1], args[5].shape[1]
    slab, ny, nz = f_cells.shape[1:]
    mort = g_mortar.shape[1]
    steps = radices(spaces)
    slots = max([regions * steps[0]] + steps)
    vmem = pl.BlockSpec(memory_space=pltpu.VMEM)
    smem = pl.BlockSpec(memory_space=pltpu.SMEM)
    field = lambda *lead: pltpu.VMEM(lead + (ny, nz), F32)
    coarse = lambda *lead: pltpu.VMEM(lead + (ny // 2, nz), F32)
    dma = lambda *shape: pltpu.SemaphoreType.DMA(shape)
    return pl.pallas_call(
        functools.partial(kernel, regions, spaces),
        out_shape=(
            jax.ShapeDtypeStruct(f_cells.shape, F32),
            jax.ShapeDtypeStruct(g_mortar.shape, F32),
        ),
        in_specs=[vmem] * 4 + [smem] + [vmem] * 4 + [smem],
        out_specs=(vmem, vmem),
        scratch_shapes=[
            field(slab + 4),
            field(slab + 4),
            field(slab + 2),
            field(slab + 2),
            field(slab + 4),
            field(slab + 2),
            field(slab + 2),
            field(ITERS + 1, slab + 4),
            field(3, slab),
            coarse(slab // 2 + 2),
            coarse(slab // 2 + 4),
            coarse(2),
            coarse(2),
            field(),
            pltpu.VMEM((3, 1, rows), F32),
            pltpu.VMEM((2, 3, 1, rows), F32),
            pltpu.VMEM(((slab + 2) * ny, 2 * mort), F32),
            pltpu.VMEM((3, regions, 1, mort), F32),
            pltpu.VMEM((ITERS, 1, mort), F32),
            pltpu.VMEM((1, mort), F32),
            pltpu.VMEM((1, mort), F32),
            pltpu.VMEM((2, len(steps), 8, 128), F32),
            pltpu.VMEM((2, len(steps), slots, 8, 128), F32),
            dma(5, 2),
            dma(5, 2),
            dma(3, regions),
            dma(3, regions),
            dma(2),
            dma(2, len(steps), slots),
            dma(2, len(steps), slots),
        ],
        compiler_params=pltpu.CompilerParams(
            collective_id=0, has_side_effects=True, vmem_limit_bytes=48 * 1024 * 1024
        ),
    )(*args)


def solution(mesh):
    in_specs = (
        P("region", "space", None, None),
        P("region", "space"),
        P("region", "space", None, None),
        P("region", "space", None, None),
        P(),
        P("space", None),
        P("space", None),
        P("space", None),
        P("space", None),
        P("space", None),
    )
    out_specs = (P("region", "space", None, None), P("region", "space"))
    return jax.shard_map(
        functools.partial(on_device, mesh.shape["region"], mesh.shape["space"]),
        mesh=mesh, in_specs=in_specs, out_specs=out_specs, check_vma=False,
    )
```

time: 1230 us -> 128 us (0.10)
  other arithmetic: 450 us -> 0 us
  blocking collectives: 412 us -> 0 us
  local copies, waits for them, and re-layouts: 186 us -> 9.25 us
  starting transfers between devices: 126 us -> 0 us
  Pallas kernels: 0 us -> 118 us
  between operations: 27.4 us -> 0.66 us
  waiting for transfers between devices: 18.5 us -> 0 us
    psum x9 -> x0, blocking collectives: 395 us -> none  [global_inner(): return lax.psum(local_inner(first, second), ('region', 'space'))]
    scatter-add x9 -> x0, other arithmetic: 133 us -> none  [the longest x4 59.3 us: on_device(): jax.ops.segment_sum(side_sign * margin_coef * paired[mort_list], own_list...]
    ppermute x38 -> x0, starting transfers between devices: 126 us -> none  [the longest x19 101 us: padded_2(): before = lax.ppermute(last, axis, up)]
    reduce_sum x18 -> x0, other arithmetic: 121 us -> none  [local_inner(): return jnp.sum(first[0] * second[0]) + jnp.sum(first[1] * second[1])]
    pallas_call x0 -> x1, Pallas kernels: none -> 118 us  [on_device(): pl.pallas_call(functools.partial(kernel, regions, spaces), out_shape=(jax...]
    mul x24 -> x0, other arithmetic: 114 us -> none  [the longest x13 104 us: fine_apply(): active * cells]
    gather x8 -> x0, local copies, waits for them, and re-layouts: 87.1 us -> none  [the longest x4 52.8 us: on_device(): paired[mort_list]]
    slice x44 -> x0, local copies, waits for them, and re-layouts: 85.5 us -> none  [the longest x12 67.8 us: coarsen(): values = values[:, :, 0::2] + values[:, :, 1::2]]
  transfers between devices with their start and end apart: 38 -> 0, of which waited for: 20 -> 0; matrix products, arithmetic and copies ran while one was open for 20% -> 0% of each run, Pallas kernels for 0% -> 0%
where the time goes in v1:
time: 128 us
  Pallas kernels  118 us (92%)
  local copies, waits for them, and re-layouts  9.25 us (7%)
    pallas_call x1, Pallas kernels, on_device(): pl.pallas_call(functools.partial(kernel, regions, spaces), out_shape=(jax...  118 us
    unnamed x22, local copies, waits for them, and re-layouts  9.25 us

profile of v1, /device:TPU:0, one launch (start us, length us, event | category | flops | bytes accessed | tf_op | source)
XLA Modules:
  0.0 127.6 jit_solution(7894389646753413146)
XLA Ops:
  0.6 0.0 copy-start
  0.6 1.0 copy-done
  1.7 0.0 copy-start.1
  1.7 1.0 copy-done.1
  2.7 0.0 copy-start.2
  2.7 1.0 copy-done.2
  3.8 0.0 copy-start.3
  3.8 0.7 copy-done.3
  4.5 0.0 copy-start.4
  4.5 0.7 copy-done.4
  5.2 0.0 copy-start.5
  5.2 0.7 copy-done.5
  5.9 0.0 copy-start.6
  5.9 0.7 copy-done.6
  6.5 0.0 copy-start.7
  6.6 0.7 copy-done.7
  7.2 0.0 copy-start.8
  7.2 0.7 copy-done.8
  7.9 0.0 copy-start.9
  7.9 0.7 copy-done.9
  8.5 117.7 %shard_map.113 = (f32[1,8,128,128]{3,2,1,0:T(8,128)S(1)}, f32[1,256]{1,0:T(1,128)S(1)}) custom-call(f32[1,8,128,128]{3,2,1,0:T(8,128)S(1)} %copy-done, f32[1,256]{1,0:T(1,128)S(1)} %copy-done.7, s32[1,8,128,128]{3,2,1,0:T(8,128)S(1)} %copy-done.1, s32[1,8,128,128]{3,2,1,0:T(8,128)S(1)} %copy-done.2, f32[16]{0:T(128)S(1)} %copy-done.8, ...), custom_call_target="tpu_custom_call" | custom-call | tf_op jit(solution)/shard_map/pallas_call | solution.py:646
  126.2 0.8 copy.14
  127.0 0.6 copy.15
Async XLA Ops:
  0.6 1.0 copy-start
  1.7 1.0 copy-start.1
  2.7 1.0 copy-start.2
  3.8 0.7 copy-start.3
  4.5 0.7 copy-start.4
  5.2 0.7 copy-start.5
  5.9 0.7 copy-start.6
  6.5 0.7 copy-start.7
  7.2 0.7 copy-start.8
  7.9 0.7 copy-start.9

commit v2 on v1

--- a/solution.py
+++ b/solution.py
@@ -28,18 +28,29 @@
 def kernel(
     regions,
     spaces,
+    f_hbm,
+    g_hbm,
+    mask_hbm,
+    zone_hbm,
+    zcoef_ref,
+    mort_hbm,
+    stokes_hbm,
+    darcy_hbm,
+    weight_hbm,
+    tiles_ref,
+    x_ref,
+    xm_ref,
     f_ref,
     g_ref,
     mask_ref,
     zone_ref,
-    zcoef_ref,
     mort_ref,
     stokes_ref,
     darcy_ref,
     weight_ref,
-    tiles_ref,
-    x_ref,
-    xm_ref,
+    in_sem,
+    one_hot,
+    lhs,
     ar,
     act,
     diag,
@@ -71,6 +82,21 @@
     red_send,
     red_recv,
 ):
+    copies = [
+        pltpu.make_async_copy(src, dst, in_sem.at[i])
+        for i, (src, dst) in enumerate((
+            (mask_hbm, mask_ref),
+            (zone_hbm, zone_ref),
+            (f_hbm, f_ref),
+            (g_hbm, g_ref),
+            (mort_hbm, mort_ref),
+            (stokes_hbm, stokes_ref),
+            (darcy_hbm, darcy_ref),
+            (weight_hbm, weight_ref),
+        ))
+    ]
+    for copy in copies:
+        copy.start()
     reg = lax.axis_index("region")
     pos = lax.axis_index("space")
     slab = f_ref.shape[1]
@@ -191,6 +217,9 @@
             value = jnp.where(ids == zone, zcoef_ref[zone], value)
         ar[l + 2] = jnp.where(mask_ref[0, l] != 0, value, 0.0)
 
+    for copy in copies:
+        copy.wait()
+
     @pl.loop(0, slab)
     def _(l):
         react_layer(l)
@@ -216,56 +245,66 @@
         q[l + 1] = f_ref[0, l]
         rs[0, l] = f_ref[0, l]
 
-    width = 256
-
     def split(value):
         high = value.astype(BF16).astype(F32)
         rest = value - high
         mid = rest.astype(BF16).astype(F32)
         return high, mid, rest - mid
 
-    def nt_dot(a, b):
-        return lax.dot_general(a, b, (((1,), (1,)), ((), ())), preferred_element_type=F32)
-
-    multiplier = lax.broadcasted_iota(jnp.int32, (2 * mort, width), 0).astype(F32)
-
-    def add_pairs(source, first_layer, layers, target, squares):
-        face = lax.broadcasted_iota(jnp.int32, (ny, width), 0).astype(F32)
-        total = jnp.zeros((8, 2 * mort), F32)
-        for chunk in range(rows // width):
-            span = pl.ds(chunk * width, width)
-            mort_row, face_row, coef_row = (source[k, :, span] for k in range(3))
-            one_hot = jnp.where(multiplier == mort_row, 1.0, 0.0).astype(BF16)
-            pieces = split(coef_row)
-
-            def body(l, carry):
-                hit = face == face_row - ((first_layer + l) * ny).astype(F32)
-                at = pl.ds(pl.multiple_of((target + l) * ny, ny), ny)
-                value = jnp.zeros((ny, 2 * mort), F32)
-                for piece in pieces:
-                    value = value + nt_dot(jnp.where(hit, piece, 0.0).astype(BF16), one_hot)
-                if chunk == 0:
-                    mx[at, :] = value
-                else:
-                    mx[at, :] = mx[at, :] + value
-                return carry
-
-            lax.fori_loop(0, layers, body, 0)
-            if squares:
-                for piece in split(coef_row * coef_row):
-                    total = total + nt_dot(
-                        jnp.broadcast_to(piece, (8, width)).astype(BF16), one_hot
-                    )
-        return total[0:1]
-
-    squares = add_pairs(meta, 0, slab, 1, True)
+    face = lax.broadcasted_iota(jnp.int32, (ny, rows), 0).astype(F32)
+    multiplier = lax.broadcasted_iota(jnp.int32, (128, 2 * mort), 1).astype(F32)
+
+    def set_one_hot(source):
+        tiles = rows // 128
+        listed = [source[0, :, pl.ds(128 * t, 128)] for t in range(tiles)]
+        listed.append(jnp.zeros((128 - tiles, 128), F32))
+        down = jnp.transpose(jnp.concatenate(listed, axis=0))
+        for t in range(tiles):
+            hit = multiplier == down[:, t : t + 1]
+            one_hot[pl.ds(128 * t, 128), :] = jnp.where(hit, 1.0, 0.0).astype(BF16)
+
+    def set_layers(source, first_layer, layers, target):
+        face_row, coef_row = source[1], source[2]
+        high, mid, _ = split(coef_row)
+        for i in range(layers):
+            start = jnp.asarray((first_layer + i) * ny, jnp.int32).astype(F32)
+            hit = face == face_row - start
+            lhs[pl.ds(2 * i * ny, ny), :] = jnp.where(hit, high, 0.0).astype(BF16)
+            lhs[pl.ds((2 * i + 1) * ny, ny), :] = jnp.where(hit, mid, 0.0).astype(BF16)
+        value = jnp.dot(
+            lhs[pl.ds(0, 2 * layers * ny), :], one_hot[...], preferred_element_type=F32
+        )
+        for i in range(layers):
+            at = (target + i) * ny
+            at = pl.ds(at if isinstance(at, int) else pl.multiple_of(at, ny), ny)
+            mx[at, :] = value[2 * i * ny : (2 * i + 1) * ny] + value[
+                (2 * i + 1) * ny : (2 * i + 2) * ny
+            ]
+
+    set_one_hot(meta)
+
+    @pl.loop(0, slab // 2)
+    def _(pair):
+        set_layers(meta, 2 * pair, 2, 1 + 2 * pair)
+
+    high, mid, low = split(meta[2] * meta[2])
+    piece = lax.broadcasted_iota(jnp.int32, (16, rows), 0)
+    pieces = jnp.where(
+        piece == 0, high, jnp.where(piece == 1, mid, jnp.where(piece == 2, low, 0.0))
+    )
+    squares = jnp.sum(
+        jnp.dot(pieces.astype(BF16), one_hot[...], preferred_element_type=F32),
+        axis=0, keepdims=True,
+    )
     own_half = lambda v: jnp.where(first_region, v[:, :mort], v[:, mort:])
     other_half = lambda v: jnp.where(first_region, v[:, mort:], v[:, :mort])
     inv_mort = 1.0 / (STAB + own_half(squares) / 3.0)
 
     wait_halo(2, meta_src, meta_dst)
-    add_pairs(metax.at[0], slab - 1, 1, 0, False)
-    add_pairs(metax.at[1], 0, 1, slab + 1, False)
+    set_one_hot(metax.at[0])
+    set_layers(metax.at[0], slab - 1, 1, 0)
+    set_one_hot(metax.at[1])
+    set_layers(metax.at[1], 0, 1, slab + 1)
     wait_halo(1, ar_src, ar_dst)
 
     @pl.loop(0, slab + 4)
@@ -354,6 +393,11 @@
     def last_layer(l):
         return 0.2 * e2[l] + inv[l] * (q[l] + act[l + 1] * neighbours(ae, l))
 
+    def finish_image():
+        @pl.loop(1, slab + 1)
+        def _(l):
+            e2[l] = last_layer(l)
+
     def fold(v):
         out = v[:, 0:128]
         for k in range(1, v.shape[1] // 128):
@@ -448,6 +492,7 @@
     lam_start(0)
     receive_coarse()
     second_all()
+    finish_image()
 
     one = jnp.ones((1, 1), F32)
     mults = [lam]
@@ -460,7 +505,7 @@
 
     def out_pass(k, scales):
         def body(l, total):
-            value = last_layer(l + 1)
+            value = e2[l + 1]
             if scales is None:
                 resid = rs[0, l]
             else:
@@ -550,12 +595,13 @@
         acc[parity, 0, 2:3] = old_row
         acc[parity, 0, 3:8] = jnp.zeros((5, 128), F32)
         red_start(parity, 0)
-        receive_coarse()
         for number in range(last_stage):
             red_next(parity, number)
+        receive_coarse()
         part_copy.wait()
         q_m = own_half(partial_rows) + part[...] - STAB * lam
         second_all()
+        finish_image()
         total = red_wait(parity, last_stage)
         sums = jnp.sum(total, axis=1, keepdims=True)
         ry, yky, yr = sums[0:1], sums[1:2], sums[2:3]
@@ -639,6 +685,7 @@
     steps = radices(spaces)
     slots = max([regions * steps[0]] + steps)
     vmem = pl.BlockSpec(memory_space=pltpu.VMEM)
+    hbm = pl.BlockSpec(memory_space=pl.ANY)
     smem = pl.BlockSpec(memory_space=pltpu.SMEM)
     field = lambda *lead: pltpu.VMEM(lead + (ny, nz), F32)
     coarse = lambda *lead: pltpu.VMEM(lead + (ny // 2, nz), F32)
@@ -649,9 +696,13 @@
             jax.ShapeDtypeStruct(f_cells.shape, F32),
             jax.ShapeDtypeStruct(g_mortar.shape, F32),
         ),
-        in_specs=[vmem] * 4 + [smem] + [vmem] * 4 + [smem],
+        in_specs=[hbm] * 4 + [smem] + [hbm] * 4 + [smem],
         out_specs=(vmem, vmem),
         scratch_shapes=[
+            *(pltpu.VMEM(args[i].shape, args[i].dtype) for i in (0, 1, 2, 3, 5, 6, 7, 8)),
+            dma(8),
+            pltpu.VMEM((rows, 2 * mort), BF16),
+            pltpu.VMEM((4 * ny, rows), BF16),
             field(slab + 4),
             field(slab + 4),
             field(slab + 2),

time: 128 us -> 107 us (0.84)
  Pallas kernels: 118 us -> 96.2 us
    pallas_call x1, Pallas kernels: 118 us -> 96.2 us  [on_device(): pl.pallas_call(functools.partial(kernel, regions, spaces), out_shape=(jax...]
where the time goes in v2:
time: 107 us; the launch traced here: 106 us
  Pallas kernels  96.2 us (90%)
  local copies, waits for them, and re-layouts  9.25 us (9%)
    pallas_call x1, Pallas kernels, on_device(): pl.pallas_call(functools.partial(kernel, regions, spaces), out_shape=(jax...  96.2 us
    unnamed x22, local copies, waits for them, and re-layouts  9.25 us

profile of v2, /device:TPU:0, one launch (start us, length us, event | category | flops | bytes accessed | tf_op | source)
XLA Modules:
  0.0 106.2 jit_solution(10187242617225064792)
XLA Ops:
  0.6 0.0 copy-start
  0.6 1.0 copy-done
  1.7 0.0 copy-start.1
  1.7 1.0 copy-done.1
  2.7 0.0 copy-start.2
  2.7 1.0 copy-done.2
  3.8 0.0 copy-start.3
  3.8 0.7 copy-done.3
  4.5 0.0 copy-start.4
  4.5 0.7 copy-done.4
  5.2 0.0 copy-start.5
  5.2 0.7 copy-done.5
  5.9 0.0 copy-start.6
  5.9 0.7 copy-done.6
  6.5 0.0 copy-start.7
  6.6 0.7 copy-done.7
  7.2 0.0 copy-start.8
  7.2 0.7 copy-done.8
  7.9 0.0 copy-start.9
  7.9 0.7 copy-done.9
  8.5 96.2 %shard_map.113 = (f32[1,8,128,128]{3,2,1,0:T(8,128)S(1)}, f32[1,256]{1,0:T(1,128)S(1)}) custom-call(f32[1,8,128,128]{3,2,1,0:T(8,128)S(1)} %copy-done, f32[1,256]{1,0:T(1,128)S(1)} %copy-done.7, s32[1,8,128,128]{3,2,1,0:T(8,128)S(1)} %copy-done.1, s32[1,8,128,128]{3,2,1,0:T(8,128)S(1)} %copy-done.2, f32[16]{0:T(128)S(1)} %copy-done.8, ...), custom_call_target="tpu_custom_call" | custom-call | tf_op jit(solution)/shard_map/pallas_call | solution.py:693
  104.8 0.8 copy.14
  105.6 0.6 copy.15
Async XLA Ops:
  0.6 1.0 copy-start
  1.7 1.0 copy-start.1
  2.7 1.0 copy-start.2
  3.8 0.7 copy-start.3
  4.5 0.7 copy-start.4
  5.2 0.7 copy-start.5
  5.9 0.7 copy-start.6
  6.5 0.7 copy-start.7
  7.2 0.7 copy-start.8
  7.9 0.7 copy-start.9

commit v3 on v2

--- a/solution.py
+++ b/solution.py
@@ -536,11 +536,14 @@
         def _(l):
             ay[l] = act[l] * ys[k, l]
 
+        @pl.loop(2, slab)
+        def _(l):
+            apply_cells(k, l)
+
         lam_wait(k)
         own_pair = paired(1, lam)
 
         def operate(l, carry):
-            apply_cells(k, l)
             add_face(l, own_pair)
             y = ys[k, l + 1]
             u = jnp.where(first_region, y[:, 0:1], y[:, nz - 1 : nz])
@@ -567,6 +570,8 @@
         wait_halo(4, y_src(k), y_dst(k))
         for l in (0, 1, slab + 2, slab + 3):
             ay[l] = act[l] * ys[k, l]
+        apply_cells(k, 1)
+        apply_cells(k, slab)
         carry = operate(jnp.int32(1), carry)
         prod, old, prt = operate(jnp.int32(slab), carry)
         apply_cells(k, 0)
@@ -685,7 +690,7 @@
     steps = radices(spaces)
     slots = max([regions * steps[0]] + steps)
     vmem = pl.BlockSpec(memory_space=pltpu.VMEM)
-    hbm = pl.BlockSpec(memory_space=pl.ANY)
+    hbm = pl.BlockSpec(memory_space=pltpu.HBM)
     smem = pl.BlockSpec(memory_space=pltpu.SMEM)
     field = lambda *lead: pltpu.VMEM(lead + (ny, nz), F32)
     coarse = lambda *lead: pltpu.VMEM(lead + (ny // 2, nz), F32)
@@ -735,7 +740,7 @@
             dma(2, len(steps), slots),
         ],
         compiler_params=pltpu.CompilerParams(
-            collective_id=0, has_side_effects=True, vmem_limit_bytes=48 * 1024 * 1024
+            collective_id=0, has_side_effects=True, vmem_limit_bytes=56 * 1024 * 1024
         ),
     )(*args)
 

time: 107 us -> 101 us (0.944)
  local copies, waits for them, and re-layouts: 9.25 us -> 2.44 us
  Pallas kernels: 96.2 us -> 97.3 us
    unnamed x22 -> x4, local copies, waits for them, and re-layouts: 9.25 us -> 2.44 us
where the time goes in v3:
time: 101 us; the launch traced here: 100 us
  Pallas kernels  97.3 us (96%)
  local copies, waits for them, and re-layouts  2.44 us (2%)
    pallas_call x1, Pallas kernels, on_device(): pl.pallas_call(functools.partial(kernel, regions, spaces), out_shape=(jax...  97.3 us
    unnamed x4, local copies, waits for them, and re-layouts  2.44 us

profile of v3, /device:TPU:0, one launch (start us, length us, event | category | flops | bytes accessed | tf_op | source)
XLA Modules:
  0.0 100.4 jit_solution(100049212673964497)
XLA Ops:
  0.6 97.3 %shard_map.113 = (f32[1,8,128,128]{3,2,1,0:T(8,128)}, f32[1,256]{1,0:T(1,128)}) custom-call(f32[1,8,128,128]{3,2,1,0:T(8,128)} %f_hbm.1, f32[1,256]{1,0:T(1,128)} %g_hbm.1, s32[1,8,128,128]{3,2,1,0:T(8,128)} %mask_hbm.1, s32[1,8,128,128]{3,2,1,0:T(8,128)} %zone_hbm.1, f32[16]{0:T(128)} %zcoef_ref.1, s32[1,2048]{1,0:T(1,128)} %mort_hbm.1, ...), custom_call_target="tpu_custom_call" | custom-call | tf_op jit(solution)/shard_map/pallas_call | solution.py:698
  97.9 0.0 copy-start
  98.0 1.9 %copy.14 = f32[1,8,128,128]{3,2,1,0:T(8,128)} copy(f32[1,8,128,128]{3,2,1,0:T(8,128)} %get-tuple-element.4) | data formatting | bytes 1048576
  99.8 0.0 copy-done
  99.8 0.6 copy.15
Async XLA Ops:
  97.9 1.9 %copy-start = (f32[1,256]{1,0:T(1,128)S(1)}, f32[1,256]{1,0:T(1,128)}, u32[]{:S(2)}) copy-start(f32[1,256]{1,0:T(1,128)} %get-tuple-element.5) | copy-start | bytes 3076
